TPU v7x, 32 devices: a whole 2x2x4 slice. The times are simulated.
32 devices in a mesh: groups: 2 (over y), rows: 16 (over z, x, core).
Axes of the slice: x: 2, y: 2, z: 4, core: 2. Of those that a mesh axis runs over, the one named last changes fastest.
Arguments:
- atmos: float32 [3, 4, 256, 1024], P(None, None, ('groups', 'rows')), parts along dimension 2, may hold values from -4 to 4
- level_set: float32 [1024, 4096], P(('groups', 'rows')), parts along dimension 0, may hold values from -8 to 8
- fuel: int32 [1024, 4096], P(('groups', 'rows')), parts along dimension 0, may hold values from 0 to 12
- fuel_table: float32 [3, 13], replicated, may hold values from 0.2 to 1
- band_home: int32 [1024, 1], P(('groups', 'rows')), parts along dimension 0, may hold values from 0 to 15; in each aligned block of 32 rows (0 to 31, 32 to 63, ...) at most 4 rows name the same one
- band_tile: int32 [1024], P(('groups', 'rows')), parts along dimension 0, may hold values from 0 to 511
Outputs:
- new_level_set: float32 [1024, 4096], P(('groups', 'rows')), parts along dimension 0
- new_atmos: float32 [3, 4, 256, 1024], P(None, None, ('groups', 'rows')), parts along dimension 2
There are 2 independent parts, one for each index of `groups`. A program takes and returns all parts, laid end to end along the dimension named above; an argument that names none is the same for every part. Nothing has to cross between parts.
Inputs may be any that keep to these rules, and one draw needn't show every extreme that they name: `band_home`: among the tiles listed on one device, at most 4 share one home block. `band_tile`: tile indices may repeat; repeated tiles add their heating.
All inputs are finite; a program needn't handle non-finite values.
Results may differ from a plain program's by a relative error of at most 0.0003.
Values sent between devices are 32-bit elements; how exact they have to be, the bound alone decides.
A program may use at most 192 MiB of HBM per device.

v0:
```python
import functools

import jax
import jax.numpy as jnp
import ml_dtypes
import numpy as np
from jax import lax
from jax.experimental import pallas as pl
from jax.experimental.pallas import tpu as pltpu
from jax.sharding import PartitionSpec as P

TILE = 64
REFINE = 16
CPT = 4
CELLS = 4096
SUBSTEPS = 4
NFUEL = 13
ROWS8 = 8
LANES = 128
SPAN = CPT + 2
PIECE = 40

fire_step = 0.1
air_step = 0.1
spread_floor = 0.01
viscosity = 0.5
mixing = 0.5
coupling = 1.0

F32 = jnp.float32
BF16 = jnp.bfloat16
HIGHEST = lax.Precision.HIGHEST


def weight_table():
    spots = (np.arange(TILE) + 0.5) / REFINE + 0.5
    nodes = np.arange(SPAN)
    return np.maximum(0.0, 1.0 - np.abs(spots[:, None] - nodes[None, :]))


def spread_weights():
    table = weight_table()
    both = np.einsum("ap,bq->qpab", table, table).reshape(SPAN * SPAN, CELLS).astype(np.float32)
    high = both.astype(ml_dtypes.bfloat16)
    low = (both - high.astype(np.float32)).astype(ml_dtypes.bfloat16)
    out = np.zeros((LANES, CELLS), ml_dtypes.bfloat16)
    for place, part in enumerate((high, high, low)):
        out[place * PIECE : place * PIECE + SPAN * SPAN] = part
    return out


def iota(shape, dim):
    return lax.broadcasted_iota(jnp.int32, shape, dim)


def halves(x):
    high = x.astype(BF16)
    return high, (x - high.astype(F32)).astype(BF16)


def dot(a, b):
    return jnp.dot(a, b, preferred_element_type=F32)


def dot_nt(a, b, precision=None):
    return lax.dot_general(
        a, b, (((1,), (1,)), ((), ())), preferred_element_type=F32, precision=precision
    )


def kernel(
    n,
    home_ref,
    tile_ref,
    table_ref,
    kron_hbm,
    atmos_hbm,
    level_hbm,
    fuel_hbm,
    newlev_hbm,
    newatm_hbm,
    kron,
    atmos,
    newatm,
    phi,
    fuel,
    rate,
    flow_r,
    flow_c,
    warm,
    acc,
    winds,
    patches,
    land,
    edge_a,
    rim_a,
    edge_b,
    rim_b,
    req,
    want,
    pick,
    back,
    heat,
    got,
    load_sem,
    save_sem,
    edge_send,
    rim_recv,
    all_send,
    all_recv,
):
    me = lax.axis_index("rows")
    slots = phi.shape[1]
    fields, levels, arows, ncols = atmos.shape
    strips = arows // CPT
    across = ncols // CPT
    cap = max(2, 2 * slots // n)
    nk = n * ROWS8

    loads = [
        pltpu.make_async_copy(src, dst, load_sem.at[i])
        for i, (src, dst) in enumerate(
            (
                (atmos_hbm, atmos),
                (fuel_hbm, fuel),
                (level_hbm, phi.at[0]),
                (kron_hbm, kron),
            )
        )
    ]
    for load in loads:
        load.start()

    rim_a[...] = jnp.zeros_like(rim_a)
    rim_b[...] = jnp.zeros_like(rim_b)

    barrier = pltpu.get_barrier_semaphore()

    def greet(d, c):
        pl.semaphore_signal(
            barrier,
            inc=1,
            device_id={"rows": lax.rem(me + d, n)},
            device_id_type=pl.DeviceIdType.MESH,
        )
        return c

    lax.fori_loop(1, n, greet, 0)

    eye = iota((slots, slots), 0) == iota((slots, slots), 1)
    earlier = iota((slots, slots), 0) < iota((slots, slots), 1)
    home_row = home_ref[...].astype(F32)
    tile_row = tile_ref[...].astype(F32)
    home_col = jnp.sum(jnp.where(eye, home_row, 0.0), axis=1, keepdims=True)
    same = (home_col == home_row) & earlier
    rank_row = jnp.sum(jnp.where(same, 1.0, 0.0), axis=0, keepdims=True)
    place_row = home_row * ROWS8 + rank_row
    place_col = jnp.sum(jnp.where(eye, place_row, 0.0), axis=1, keepdims=True)
    placing_t = iota((nk, slots), 0).astype(F32) == place_row
    placing = jnp.where(place_col == iota((slots, nk), 1).astype(F32), 1.0, 0.0).astype(BF16)
    asked = jnp.sum(jnp.where(placing_t, tile_row, 0.0), axis=1, keepdims=True)
    req[...] = jnp.broadcast_to(asked, (nk, LANES))

    loads[0].wait()
    for side, row in ((0, arows - 1), (1, 0)):
        for f in range(2):
            edge_a[side, f : f + 1, :] = atmos[f, 0, row : row + 1, :]
        for f in range(fields):
            for k in range(levels):
                at = f * levels + k
                edge_b[side, at : at + 1, :] = atmos[f, k, row : row + 1, :]

    pl.semaphore_wait(barrier, n - 1)

    def edge_copy(side, which):
        src, dst = ((edge_a, rim_a), (edge_b, rim_b))[which]
        return pltpu.make_async_remote_copy(
            src_ref=src.at[side],
            dst_ref=dst.at[side],
            send_sem=edge_send.at[which, side],
            recv_sem=rim_recv.at[which, side],
            device_id={"rows": jnp.clip(me + (1 - 2 * side), 0, n - 1)},
            device_id_type=pl.DeviceIdType.MESH,
        )

    def send_edges(which):
        @pl.when(me < n - 1)
        def _():
            edge_copy(0, which).start()

        @pl.when(me > 0)
        def _():
            edge_copy(1, which).start()

    def recv_edges(which):
        @pl.when(me > 0)
        def _():
            edge_copy(0, which).wait_recv()

        @pl.when(me < n - 1)
        def _():
            edge_copy(1, which).wait_recv()

    def sent_edges(which):
        @pl.when(me < n - 1)
        def _():
            edge_copy(0, which).wait_send()

        @pl.when(me > 0)
        def _():
            edge_copy(1, which).wait_send()

    mine = pl.ds(pl.multiple_of(me * ROWS8, ROWS8), ROWS8)

    def exchange(src, dst, number):
        def send(d, c):
            peer = lax.rem(me + d, n)
            pltpu.make_async_remote_copy(
                src_ref=src.at[pl.ds(pl.multiple_of(peer * ROWS8, ROWS8), ROWS8)],
                dst_ref=dst.at[mine],
                send_sem=all_send.at[number],
                recv_sem=all_recv.at[number],
                device_id={"rows": peer},
                device_id_type=pl.DeviceIdType.MESH,
            ).start()
            return c

        lax.fori_loop(1, n, send, 0)

    def arrive(src, dst, number):
        others = pl.ds(0, (n - 1) * ROWS8)
        pltpu.make_async_copy(dst.at[others], dst.at[others], all_recv.at[number]).wait()
        dst[mine, :] = src[mine, :]

    def gone(src, number):
        others = pl.ds(0, (n - 1) * ROWS8)
        pltpu.make_async_copy(src.at[others], src.at[others], all_send.at[number]).wait()

    send_edges(0)
    exchange(req, want, 0)
    send_edges(1)

    loads[1].wait()

    def params(v, c):
        cols = pl.ds(pl.multiple_of(v * LANES, LANES), LANES)
        kinds = fuel[:, cols]
        bits = [(kinds & (1 << b)) != 0 for b in range(4)]
        for row, (ref, scale) in enumerate(((rate, fire_step), (flow_r, fire_step), (warm, 1.0))):
            vals = [table_ref[row, i] * scale for i in range(NFUEL)]
            for bit in bits:
                nxt = []
                for i in range(0, len(vals), 2):
                    if i + 1 < len(vals):
                        nxt.append(jnp.where(bit, vals[i + 1], vals[i]))
                    else:
                        nxt.append(vals[i])
                vals = nxt
            ref[:, cols] = vals[0]
        acc[:, cols] = jnp.zeros((slots, LANES), F32)
        return c

    lax.fori_loop(0, CELLS // LANES, params, 0)

    recv_edges(0)
    for f in range(2):
        winds[f, 0:1, :] = rim_a[0, f : f + 1, :]
        winds[f, 1 : 1 + arows, :] = atmos[f, 0]
        winds[f, 1 + arows : 2 + arows, :] = rim_a[1, f : f + 1, :]
        winds[f, 2 + arows : 8 + arows, :] = jnp.zeros((6, ncols), F32)
    col8 = iota((ROWS8, ncols), 1)
    patches[...] = jnp.zeros_like(patches)
    for f in range(2):
        for strip in range(strips):
            base = winds[f, strip * CPT : strip * CPT + ROWS8, :]
            for q in range(SPAN):
                moved = base if q == 1 else pltpu.roll(base, (1 - q) % ncols, axis=1)
                if q == 0:
                    moved = jnp.where(col8 == 0, 0.0, moved)
                if q == SPAN - 1:
                    moved = jnp.where(col8 >= ncols - CPT, 0.0, moved)
                at = f * 64 + q * SPAN
                patches[at : at + SPAN, strip * ncols : (strip + 1) * ncols] = moved[:SPAN]
    table_high, table_low = halves(patches[...])

    arrive(req, want, 0)
    for chunk in range(0, nk, LANES):
        t = want[chunk : chunk + LANES, 0:1]
        hot = jnp.where(
            iota((LANES, strips * ncols), 1).astype(F32) == CPT * t, 1.0, 0.0
        ).astype(BF16)
        pick[chunk : chunk + LANES, :] = dot_nt(hot, table_high) + dot_nt(hot, table_low)
    exchange(pick, back, 1)

    for chunk in range(0, nk, LANES):
        t = want[chunk : chunk + LANES, 0:1]
        for strip in range(1, strips):
            t = jnp.where(t >= across, t - across, t)
        group = (iota((LANES, ncols), 1) // CPT).astype(F32)
        land[chunk : chunk + LANES, :] = jnp.where(group == t, 1.0, 0.0).astype(BF16)

    recv_edges(1)
    row8 = iota((arows, ncols), 0)
    colx = iota((arows, ncols), 1)
    for k in range(levels):
        wind_r = atmos[0, k] * (0.5 * air_step)
        wind_c = atmos[1, k] * (0.5 * air_step)
        for f in range(fields):
            at = f * levels + k
            centre = atmos[f, k]
            north = jnp.where(row8 == 0, rim_b[0, at : at + 1, :], pltpu.roll(centre, 1, axis=0))
            south = jnp.where(
                row8 == arows - 1, rim_b[1, at : at + 1, :], pltpu.roll(centre, arows - 1, axis=0)
            )
            west = jnp.where(colx == 0, 0.0, pltpu.roll(centre, 1, axis=1))
            east = jnp.where(colx == ncols - 1, 0.0, pltpu.roll(centre, ncols - 1, axis=1))
            above = atmos[f, min(k + 1, levels - 1)]
            below = atmos[f, max(k - 1, 0)]
            laplace = north + south + west + east - 4.0 * centre
            vertical = above + below - 2.0 * centre
            carried = wind_r * (south - north) + wind_c * (east - west)
            newatm[f, k] = (
                centre
                + (air_step * viscosity) * laplace
                + (air_step * mixing) * vertical
                - carried
            )

    loads[3].wait()
    arrive(pick, back, 1)
    back_high, back_low = halves(back[...])
    own_high = dot(placing, back_high)
    own_low = dot(placing, back_low)
    lane = iota((slots, LANES), 1)

    def field_rows(x):
        first = jnp.where(lane < 64, x, 0.0)
        second = jnp.where(lane < 64, pltpu.roll(x, 64, axis=1), 0.0)
        return jnp.concatenate([first, second], axis=0)

    high, low = field_rows(own_high), field_rows(own_low)
    left = (high + pltpu.roll(low, PIECE, axis=1) + pltpu.roll(high, 2 * PIECE, axis=1)).astype(
        BF16
    )

    def blow(v, c):
        cols = pl.ds(pl.multiple_of(v * 512, 512), 512)
        wind = dot(left, kron[:, cols])
        reach = flow_r[:, cols]
        flow_r[:, cols] = reach * wind[:slots]
        flow_c[:, cols] = reach * wind[slots:]
        return c

    lax.fori_loop(0, CELLS // 512, blow, 0)

    loads[2].wait()
    top_half = lane < TILE
    first_col = (lane & (TILE - 1)) == 0
    columns = CELLS // LANES

    def substep(step, c):
        now = lax.rem(step, 2)
        later = 1 - now

        def cell(v):
            return phi[now, :, v * LANES : (v + 1) * LANES]

        centre = cell(0)
        turned = pltpu.roll(centre, TILE, axis=1)
        before = centre
        for v in range(columns):
            cols = slice(v * LANES, (v + 1) * LANES)
            if v + 1 < columns:
                ahead = cell(v + 1)
                ahead_turned = pltpu.roll(ahead, TILE, axis=1)
            else:
                ahead, ahead_turned = None, centre
            prev = jnp.where(top_half, before, turned)
            nxt = jnp.where(top_half, turned, ahead_turned)
            back_r = centre - prev
            ahead_r = nxt - centre
            back_c = jnp.where(first_col, 0.0, centre - pltpu.roll(centre, 1, axis=1))
            ahead_c = pltpu.roll(back_c, LANES - 1, axis=1)
            a = jnp.maximum(back_r, 0.0)
            b = jnp.minimum(ahead_r, 0.0)
            d = jnp.maximum(back_c, 0.0)
            e = jnp.minimum(ahead_c, 0.0)
            slope = (a * a + b * b) + (d * d + e * e) + spread_floor
            fr = flow_r[:, cols]
            fc = flow_c[:, cols]
            move = fr * jnp.where(fr > 0.0, back_r, ahead_r) + fc * jnp.where(
                fc > 0.0, back_c, ahead_c
            )
            new = centre - (rate[:, cols] * (slope * lax.rsqrt(slope)) + move)
            phi[later, :, cols] = new
            acc[:, cols] += jnp.exp(-(new * new))
            before, centre, turned = turned, ahead, ahead_turned
        return c

    lax.fori_loop(0, SUBSTEPS, substep, 0)

    saves = [
        pltpu.make_async_copy(phi.at[0], newlev_hbm, save_sem.at[0]),
        pltpu.make_async_copy(newatm, newatm_hbm, save_sem.at[1]),
    ]
    saves[0].start()

    per = columns // CPT
    total = jnp.zeros((slots, LANES), F32)
    for i in range(CPT):
        part = jnp.zeros((slots, LANES), F32)
        for v in range(i * per, (i + 1) * per):
            cols = slice(v * LANES, (v + 1) * LANES)
            part = part + acc[:, cols] * warm[:, cols]
        source = iota((LANES, LANES), 0)
        target = iota((LANES, LANES), 1)
        mean = jnp.where(
            (source & (TILE - 1)) // REFINE + i * CPT == target,
            1.0 / (SUBSTEPS * REFINE * REFINE),
            0.0,
        ).astype(BF16)
        part_high, part_low = halves(part)
        total = total + dot(part_high, mean) + dot(part_low, mean)
    total_high, total_low = halves(total)
    out_of = jnp.where(placing_t, 1.0, 0.0).astype(BF16)
    heat[...] = dot(out_of, total_high) + dot(out_of, total_low)
    exchange(heat, got, 2)
    sent_edges(0)
    sent_edges(1)
    gone(req, 0)
    gone(pick, 1)
    arrive(heat, got, 2)

    spots = CPT * arows
    ranks = iota((spots, LANES), 0)
    r = ranks & (arows - 1)
    wanted_lane = (r // CPT) * (CPT * CPT) + (r % CPT) * CPT + ranks // arows
    choose = jnp.where(iota((spots, LANES), 1) == wanted_lane, 1.0, 0.0).astype(BF16)
    landed = jnp.zeros((2 * spots, ncols), F32)
    for chunk in range(0, nk, LANES):
        rows = slice(chunk, chunk + LANES)
        t = want[rows, :]
        x = got[rows, :]
        spread = jnp.zeros((LANES, LANES), F32)
        for strip in range(strips):
            here = (t >= strip * across) & (t < (strip + 1) * across)
            part = jnp.where(here, x, 0.0)
            if strip:
                part = pltpu.roll(part, strip * CPT * CPT, axis=1)
            spread = spread + part
        s_high, s_low = halves(spread)
        both = jnp.concatenate([dot_nt(choose, s_high), dot_nt(choose, s_low)], axis=0)
        landed = landed + dot(both.astype(BF16), land[rows, :])
    landed = landed[:spots] + landed[spots:]
    turn = colx & (CPT - 1)
    heating = landed[:arows]
    for j in range(1, CPT):
        heating = jnp.where(turn == j, landed[j * arows : (j + 1) * arows], heating)
    newatm[2, 0] = newatm[2, 0] + coupling * heating
    saves[1].start()
    gone(heat, 2)
    saves[0].wait()
    saves[1].wait()


def shards(n, atmos, level_set, fuel, fuel_table, band_home, band_tile):
    slots = level_set.shape[0]
    fields, levels, arows, ncols = atmos.shape
    nk = n * ROWS8
    cells = (slots, CELLS)
    vmem = pltpu.VMEM
    hbm = pl.BlockSpec(memory_space=pl.ANY)
    local = pl.BlockSpec(memory_space=pltpu.VMEM)
    kron = jnp.asarray(spread_weights())
    return pl.pallas_call(
        functools.partial(kernel, n),
        out_shape=(
            jax.ShapeDtypeStruct(level_set.shape, F32),
            jax.ShapeDtypeStruct(atmos.shape, F32),
        ),
        in_specs=[local, local, pl.BlockSpec(memory_space=pltpu.SMEM), hbm, hbm, hbm, hbm],
        out_specs=(hbm, hbm),
        scratch_shapes=[
            vmem((LANES, CELLS), BF16),
            vmem(atmos.shape, F32),
            vmem(atmos.shape, F32),
            vmem((2,) + cells, F32),
            vmem(cells, jnp.int32),
            vmem(cells, F32),
            vmem(cells, F32),
            vmem(cells, F32),
            vmem(cells, F32),
            vmem(cells, F32),
            vmem((2, arows + 8, ncols), F32),
            vmem((LANES, arows // CPT * ncols), F32),
            vmem((nk, ncols), BF16),
            vmem((2, 2, ncols), F32),
            vmem((2, 2, ncols), F32),
            vmem((2, fields * levels, ncols), F32),
            vmem((2, fields * levels, ncols), F32),
        ]
        + [vmem((nk, LANES), F32)] * 6
        + [
            pltpu.SemaphoreType.DMA((4,)),
            pltpu.SemaphoreType.DMA((2,)),
            pltpu.SemaphoreType.DMA((2, 2)),
            pltpu.SemaphoreType.DMA((2, 2)),
            pltpu.SemaphoreType.DMA((3,)),
            pltpu.SemaphoreType.DMA((3,)),
        ],
        compiler_params=pltpu.CompilerParams(
            collective_id=0, has_side_effects=True, vmem_limit_bytes=48 * 1024 * 1024
        ),
    )(
        band_home.reshape(1, slots),
        band_tile.reshape(1, slots),
        fuel_table,
        kron,
        atmos,
        level_set,
        fuel,
    )


def solution(mesh):
    placed = (
        P(None, None, ("groups", "rows"), None),
        P(("groups", "rows"), None),
        P(("groups", "rows"), None),
        P(),
        P(("groups", "rows"), None),
        P(("groups", "rows")),
    )
    return jax.shard_map(
        functools.partial(shards, mesh.shape["rows"]),
        mesh=mesh,
        in_specs=placed,
        out_specs=(P(("groups", "rows"), None), P(None, None, ("groups", "rows"), None)),
        check_vma=False,
    )
```

profile of v0, /device:TPU:0, one launch (start us, length us, event | category | flops | bytes accessed | tf_op | source)
XLA Modules:
  0.0 36.8 jit_solution(7026586672479457415)
XLA Ops:
  0.6 0.0 copy-start.4
  0.6 0.0 copy-start.5
  0.7 0.0 copy-start.6
  0.7 0.7 %copy-done.4 = f32[3,13]{1,0:T(4,128)S(1)} copy-done((f32[3,13]{1,0:T(4,128)S(1)}, f32[3,13]{1,0:T(4,128)}, u32[]{:S(2)}) %copy-start.4) | copy-done | bytes 180
  1.3 0.0 copy-done.5
  1.3 0.0 copy-done.6
  1.3 0.0 copy-start
  1.3 1.2 %copy-done = bf16[128,4096]{1,0:T(8,128)(2,1)S(1)} copy-done((bf16[128,4096]{1,0:T(8,128)(2,1)S(1)}, bf16[128,4096]{1,0:T(8,128)(2,1)}, u32[]{:S(2)}) %copy-start) | copy-done | bytes 1048600
  2.5 0.0 copy-start.1
  2.5 1.0 %copy-done.1 = f32[32,4096]{1,0:T(8,128)S(1)} copy-done((f32[32,4096]{1,0:T(8,128)S(1)}, f32[32,4096]{1,0:T(8,128)}, u32[]{:S(2)}) %copy-start.1) | copy-done | bytes 524312
  3.6 0.0 copy-start.2
  3.6 1.0 %copy-done.2 = s32[32,4096]{1,0:T(8,128)S(1)} copy-done((s32[32,4096]{1,0:T(8,128)S(1)}, s32[32,4096]{1,0:T(8,128)}, u32[]{:S(2)}) %copy-start.2) | copy-done | bytes 524312
  4.6 0.0 copy-start.3
  4.6 1.0 %copy-done.3 = f32[3,4,8,1024]{3,2,1,0:T(8,128)S(1)} copy-done((f32[3,4,8,1024]{3,2,1,0:T(8,128)S(1)}, f32[3,4,8,1024]{3,2,1,0:T(8,128)}, u32[]{:S(2)}) %copy-start.3) | copy-done | bytes 393240
  5.6 29.6 %shard_map.86 = (f32[32,4096]{1,0:T(8,128)S(1)}, f32[3,4,8,1024]{3,2,1,0:T(8,128)S(1)}) custom-call(s32[1,32]{1,0:T(1,128)S(1)} %bitcast.2, s32[1,32]{1,0:T(1,128)S(1)} %bitcast.3, f32[3,13]{1,0:T(4,128)S(1)} %copy-done.4, bf16[128,4096]{1,0:T(8,128)(2,1)S(1)} %copy-done, f32[3,4,8,1024]{3,2,1,0:T(8,128)S(1)} %copy-done.3, f32[32,4096]{1,0:T(8,128)S(1)} %copy-done.1, ...), custom_call_target="tpu_custom_call" | custom-call | tf_op jit(solution)/shard_map/pallas_call | solution.py:475
  35.3 0.8 %copy.11 = f32[32,4096]{1,0:T(8,128)} copy(f32[32,4096]{1,0:T(8,128)S(1)} %get-tuple-element.4) | data formatting | bytes 1048576
  36.1 0.7 %copy.12 = f32[3,4,8,1024]{3,2,1,0:T(8,128)} copy(f32[3,4,8,1024]{3,2,1,0:T(8,128)S(1)} %get-tuple-element.5) | data formatting | bytes 786432
Async XLA Ops:
  0.6 0.7 %copy-start.4 = (f32[3,13]{1,0:T(4,128)S(1)}, f32[3,13]{1,0:T(4,128)}, u32[]{:S(2)}) copy-start(f32[3,13]{1,0:T(4,128)} %table_ref.1) | copy-start | bytes 472
  0.6 0.7 %copy-start.5 = (s32[32,1]{0,1:T(1,128)S(1)}, s32[32,1]{0,1:T(1,128)}, u32[]{:S(2)}) copy-start(s32[32,1]{0,1:T(1,128)} %param.11) | copy-start | bytes 388
  0.7 0.7 %copy-start.6 = (s32[32]{0:T(128)S(1)}, s32[32]{0:T(128)}, u32[]{:S(2)}) copy-start(s32[32]{0:T(128)} %param.12) | copy-start | bytes 388
  1.3 1.2 %copy-start = (bf16[128,4096]{1,0:T(8,128)(2,1)S(1)}, bf16[128,4096]{1,0:T(8,128)(2,1)}, u32[]{:S(2)}) copy-start(bf16[128,4096]{1,0:T(8,128)(2,1)} %constant.2.clone.kron_hbm) | copy-start | bytes 3145732
  2.5 1.0 %copy-start.1 = (f32[32,4096]{1,0:T(8,128)S(1)}, f32[32,4096]{1,0:T(8,128)}, u32[]{:S(2)}) copy-start(f32[32,4096]{1,0:T(8,128)} %level_hbm.1) | copy-start | bytes 1572868
  3.6 1.0 %copy-start.2 = (s32[32,4096]{1,0:T(8,128)S(1)}, s32[32,4096]{1,0:T(8,128)}, u32[]{:S(2)}) copy-start(s32[32,4096]{1,0:T(8,128)} %fuel_hbm.1) | copy-start | bytes 1572868
  4.6 1.0 %copy-start.3 = (f32[3,4,8,1024]{3,2,1,0:T(8,128)S(1)}, f32[3,4,8,1024]{3,2,1,0:T(8,128)}, u32[]{:S(2)}) copy-start(f32[3,4,8,1024]{3,2,1,0:T(8,128)} %atmos_hbm.1) | copy-start | bytes 1179652
where the time goes:
time: 37.1 us; the launch traced here: 36.8 us
  Pallas kernels  29.6 us (80%)
  local copies, waits for them, and re-layouts  6.51 us (18%)
  between operations  0.67 us (2%)
    pallas_call x1, Pallas kernels, shards(): pl.pallas_call(functools.partial(kernel, n), out_shape=(jax.ShapeDtypeStr...  29.6 us
    unnamed x16, local copies, waits for them, and re-layouts  6.51 us

commit v1 on v0

--- a/solution.py
+++ b/solution.py
@@ -40,13 +40,26 @@
 
 def spread_weights():
     table = weight_table()
-    both = np.einsum("ap,bq->qpab", table, table).reshape(SPAN * SPAN, CELLS).astype(np.float32)
-    high = both.astype(ml_dtypes.bfloat16)
-    low = (both - high.astype(np.float32)).astype(ml_dtypes.bfloat16)
-    out = np.zeros((LANES, CELLS), ml_dtypes.bfloat16)
-    for place, part in enumerate((high, high, low)):
-        out[place * PIECE : place * PIECE + SPAN * SPAN] = part
-    return out
+    out = np.zeros((2, LANES, SPAN, LANES), ml_dtypes.bfloat16)
+    for half in range(2):
+        for part in range(2):
+            for q in range(SPAN):
+                for p in range(SPAN):
+                    at = part * PIECE + q * SPAN + p
+                    out[half, at, p, half * TILE : (half + 1) * TILE] = table[:, q]
+    return out.reshape(2 * LANES, SPAN * LANES)
+
+
+def side_weights():
+    out = np.zeros((2, LANES, 2, LANES), ml_dtypes.bfloat16)
+    for b in range(LANES):
+        if b % TILE:
+            out[:, b, 0, b] = 1
+            out[:, b - 1, 0, b] = -1
+        if (b + 1) % TILE:
+            out[:, b + 1, 1, b] = 1
+            out[:, b, 1, b] = -1
+    return out.reshape(2 * LANES, 2 * LANES)
 
 
 def iota(shape, dim):
@@ -73,18 +86,23 @@
     home_ref,
     tile_ref,
     table_ref,
-    kron_hbm,
+    spread_hbm,
+    sides_hbm,
     atmos_hbm,
     level_hbm,
     fuel_hbm,
     newlev_hbm,
     newatm_hbm,
-    kron,
+    spread,
+    sides,
     atmos,
     newatm,
-    phi,
+    level,
+    phi_a,
+    phi_b,
     fuel,
     rate,
+    reach,
     flow_r,
     flow_c,
     warm,
@@ -110,7 +128,8 @@
     all_recv,
 ):
     me = lax.axis_index("rows")
-    slots = phi.shape[1]
+    slots = level.shape[0]
+    pairs = slots // 2
     fields, levels, arows, ncols = atmos.shape
     strips = arows // CPT
     across = ncols // CPT
@@ -123,8 +142,9 @@
             (
                 (atmos_hbm, atmos),
                 (fuel_hbm, fuel),
-                (level_hbm, phi.at[0]),
-                (kron_hbm, kron),
+                (level_hbm, level),
+                (spread_hbm, spread),
+                (sides_hbm, sides),
             )
         )
     ]
@@ -242,22 +262,32 @@
 
     loads[1].wait()
 
+    low_half = iota((pairs, LANES), 1) < TILE
+
+    def swap(x, y):
+        turned_x = pltpu.roll(x, TILE, axis=1)
+        turned_y = pltpu.roll(y, TILE, axis=1)
+        return jnp.where(low_half, x, turned_y), jnp.where(low_half, turned_x, y)
+
+    def narrow(v):
+        return pl.ds(pl.multiple_of(v * LANES, LANES), LANES)
+
     def params(v, c):
-        cols = pl.ds(pl.multiple_of(v * LANES, LANES), LANES)
-        kinds = fuel[:, cols]
-        bits = [(kinds & (1 << b)) != 0 for b in range(4)]
-        for row, (ref, scale) in enumerate(((rate, fire_step), (flow_r, fire_step), (warm, 1.0))):
-            vals = [table_ref[row, i] * scale for i in range(NFUEL)]
-            for bit in bits:
-                nxt = []
-                for i in range(0, len(vals), 2):
-                    if i + 1 < len(vals):
-                        nxt.append(jnp.where(bit, vals[i + 1], vals[i]))
-                    else:
-                        nxt.append(vals[i])
-                vals = nxt
-            ref[:, cols] = vals[0]
-        acc[:, cols] = jnp.zeros((slots, LANES), F32)
+        both = swap(fuel[:pairs, narrow(v)], fuel[pairs:, narrow(v)])
+        for half in range(2):
+            cols = narrow(2 * v + half)
+            bits = [(both[half] & (1 << b)) != 0 for b in range(4)]
+            for row, (ref, scale) in enumerate(
+                ((rate, fire_step), (reach, fire_step), (warm, 1.0))
+            ):
+                vals = [table_ref[row, i] * scale for i in range(NFUEL)]
+                for bit in bits:
+                    vals = [
+                        jnp.where(bit, vals[i + 1], vals[i]) if i + 1 < len(vals) else vals[i]
+                        for i in range(0, len(vals), 2)
+                    ]
+                ref[:, cols] = vals[0]
+            acc[:, cols] = jnp.zeros((pairs, LANES), F32)
         return c
 
     lax.fori_loop(0, CELLS // LANES, params, 0)
@@ -299,10 +329,9 @@
         group = (iota((LANES, ncols), 1) // CPT).astype(F32)
         land[chunk : chunk + LANES, :] = jnp.where(group == t, 1.0, 0.0).astype(BF16)
 
-    recv_edges(1)
     row8 = iota((arows, ncols), 0)
     colx = iota((arows, ncols), 1)
-    for k in range(levels):
+    def air(k):
         wind_r = atmos[0, k] * (0.5 * air_step)
         wind_c = atmos[1, k] * (0.5 * air_step)
         for f in range(fields):
@@ -326,105 +355,120 @@
                 - carried
             )
 
+    loads[2].wait()
+
+    def pack(v, c):
+        first, second = swap(level[:pairs, narrow(v)], level[pairs:, narrow(v)])
+        phi_a[:, narrow(2 * v)] = first
+        phi_a[:, narrow(2 * v + 1)] = second
+        return c
+
+    lax.fori_loop(0, CELLS // LANES, pack, 0)
+    recv_edges(1)
+    for k in range(levels // 2, levels):
+        air(k)
+
     loads[3].wait()
     arrive(pick, back, 1)
     back_high, back_low = halves(back[...])
     own_high = dot(placing, back_high)
     own_low = dot(placing, back_low)
     lane = iota((slots, LANES), 1)
-
-    def field_rows(x):
-        first = jnp.where(lane < 64, x, 0.0)
-        second = jnp.where(lane < 64, pltpu.roll(x, 64, axis=1), 0.0)
-        return jnp.concatenate([first, second], axis=0)
-
-    high, low = field_rows(own_high), field_rows(own_low)
-    left = (high + pltpu.roll(low, PIECE, axis=1) + pltpu.roll(high, 2 * PIECE, axis=1)).astype(
-        BF16
+    ahead_parts = []
+    for f in range(2):
+        high, low = own_high, own_low
+        if f:
+            high, low = pltpu.roll(high, 64, axis=1), pltpu.roll(low, 64, axis=1)
+        high, low = jnp.where(lane < PIECE, high, 0.0), jnp.where(lane < PIECE, low, 0.0)
+        ahead_parts.append((high + pltpu.roll(low, PIECE, axis=1)).astype(BF16))
+    left = jnp.concatenate(
+        [jnp.concatenate([x[:pairs], x[pairs:]], axis=1) for x in ahead_parts], axis=0
     )
-
-    def blow(v, c):
-        cols = pl.ds(pl.multiple_of(v * 512, 512), 512)
-        wind = dot(left, kron[:, cols])
-        reach = flow_r[:, cols]
-        flow_r[:, cols] = reach * wind[:slots]
-        flow_c[:, cols] = reach * wind[slots:]
+    along = dot(left, spread[...])
+    table = weight_table()
+    for f, ref in enumerate((flow_r, flow_c)):
+        nodes = [along[f * pairs : (f + 1) * pairs, p * LANES : (p + 1) * LANES] for p in range(SPAN)]
+        for a in range(TILE):
+            cols = slice(a * LANES, (a + 1) * LANES)
+            wind = sum(float(table[a, p]) * nodes[p] for p in range(SPAN) if table[a, p])
+            ref[:, cols] = reach[:, cols] * wind
+
+    loads[4].wait()
+    sides_table = sides[...]
+    batch = 8
+
+    def substep(now, later):
+        def row(i):
+            return now[:, i * LANES : (i + 1) * LANES]
+
+        for start in range(0, TILE, batch):
+            split = [halves(row(i)) for i in range(start, start + batch)]
+            parts = jnp.concatenate([jnp.concatenate(x, axis=1) for x in split], axis=0)
+            across_cols = dot(parts, sides_table)
+            centre = row(start)
+            back_r = jnp.zeros_like(centre) if start == 0 else centre - row(start - 1)
+            for i in range(start, start + batch):
+                cols = slice(i * LANES, (i + 1) * LANES)
+                here = slice((i - start) * pairs, (i - start + 1) * pairs)
+                back_c = across_cols[here, :LANES]
+                ahead_c = across_cols[here, LANES:]
+                following = row(i + 1) if i + 1 < TILE else centre
+                ahead_r = following - centre
+                a = jnp.maximum(back_r, 0.0)
+                b = jnp.minimum(ahead_r, 0.0)
+                d = jnp.maximum(back_c, 0.0)
+                e = jnp.minimum(ahead_c, 0.0)
+                slope = (a * a + b * b) + (d * d + e * e) + spread_floor
+                fr = flow_r[:, cols]
+                fc = flow_c[:, cols]
+                move = fr * jnp.where(fr > 0.0, back_r, ahead_r) + fc * jnp.where(
+                    fc > 0.0, back_c, ahead_c
+                )
+                new = centre - (rate[:, cols] * (slope * lax.rsqrt(slope)) + move)
+                later[:, cols] = new
+                acc[:, cols] += jnp.exp(-(new * new))
+                centre, back_r = following, ahead_r
+
+    def two_substeps(pair, c):
+        substep(phi_a, phi_b)
+        substep(phi_b, phi_a)
         return c
 
-    lax.fori_loop(0, CELLS // 512, blow, 0)
-
-    loads[2].wait()
-    top_half = lane < TILE
-    first_col = (lane & (TILE - 1)) == 0
-    columns = CELLS // LANES
-
-    def substep(step, c):
-        now = lax.rem(step, 2)
-        later = 1 - now
-
-        def cell(v):
-            return phi[now, :, v * LANES : (v + 1) * LANES]
-
-        centre = cell(0)
-        turned = pltpu.roll(centre, TILE, axis=1)
-        before = centre
-        for v in range(columns):
-            cols = slice(v * LANES, (v + 1) * LANES)
-            if v + 1 < columns:
-                ahead = cell(v + 1)
-                ahead_turned = pltpu.roll(ahead, TILE, axis=1)
-            else:
-                ahead, ahead_turned = None, centre
-            prev = jnp.where(top_half, before, turned)
-            nxt = jnp.where(top_half, turned, ahead_turned)
-            back_r = centre - prev
-            ahead_r = nxt - centre
-            back_c = jnp.where(first_col, 0.0, centre - pltpu.roll(centre, 1, axis=1))
-            ahead_c = pltpu.roll(back_c, LANES - 1, axis=1)
-            a = jnp.maximum(back_r, 0.0)
-            b = jnp.minimum(ahead_r, 0.0)
-            d = jnp.maximum(back_c, 0.0)
-            e = jnp.minimum(ahead_c, 0.0)
-            slope = (a * a + b * b) + (d * d + e * e) + spread_floor
-            fr = flow_r[:, cols]
-            fc = flow_c[:, cols]
-            move = fr * jnp.where(fr > 0.0, back_r, ahead_r) + fc * jnp.where(
-                fc > 0.0, back_c, ahead_c
-            )
-            new = centre - (rate[:, cols] * (slope * lax.rsqrt(slope)) + move)
-            phi[later, :, cols] = new
-            acc[:, cols] += jnp.exp(-(new * new))
-            before, centre, turned = turned, ahead, ahead_turned
-        return c
-
-    lax.fori_loop(0, SUBSTEPS, substep, 0)
+    lax.fori_loop(0, SUBSTEPS // 2, two_substeps, 0)
 
     saves = [
-        pltpu.make_async_copy(phi.at[0], newlev_hbm, save_sem.at[0]),
+        pltpu.make_async_copy(level, newlev_hbm, save_sem.at[0]),
         pltpu.make_async_copy(newatm, newatm_hbm, save_sem.at[1]),
     ]
-    saves[0].start()
-
-    per = columns // CPT
-    total = jnp.zeros((slots, LANES), F32)
+
+    total = jnp.zeros((pairs, 2 * LANES), F32)
     for i in range(CPT):
-        part = jnp.zeros((slots, LANES), F32)
-        for v in range(i * per, (i + 1) * per):
-            cols = slice(v * LANES, (v + 1) * LANES)
+        part = jnp.zeros((pairs, LANES), F32)
+        for a in range(i * REFINE, (i + 1) * REFINE):
+            cols = slice(a * LANES, (a + 1) * LANES)
             part = part + acc[:, cols] * warm[:, cols]
-        source = iota((LANES, LANES), 0)
-        target = iota((LANES, LANES), 1)
-        mean = jnp.where(
-            (source & (TILE - 1)) // REFINE + i * CPT == target,
-            1.0 / (SUBSTEPS * REFINE * REFINE),
-            0.0,
-        ).astype(BF16)
+        source = iota((LANES, 2 * LANES), 0)
+        target = iota((LANES, 2 * LANES), 1)
+        spot = (source // TILE) * LANES + (source & (TILE - 1)) // REFINE + i * CPT
+        mean = jnp.where(spot == target, 1.0 / (SUBSTEPS * REFINE * REFINE), 0.0).astype(BF16)
         part_high, part_low = halves(part)
         total = total + dot(part_high, mean) + dot(part_low, mean)
+    total = jnp.concatenate([total[:, :LANES], total[:, LANES:]], axis=0)
     total_high, total_low = halves(total)
     out_of = jnp.where(placing_t, 1.0, 0.0).astype(BF16)
     heat[...] = dot(out_of, total_high) + dot(out_of, total_low)
     exchange(heat, got, 2)
+
+    def unpack(v, c):
+        first, second = swap(phi_a[:, narrow(2 * v)], phi_a[:, narrow(2 * v + 1)])
+        level[:pairs, narrow(v)] = first
+        level[pairs:, narrow(v)] = second
+        return c
+
+    lax.fori_loop(0, CELLS // LANES, unpack, 0)
+    saves[0].start()
+    for k in range(levels // 2):
+        air(k)
     sent_edges(0)
     sent_edges(1)
     gone(req, 0)
@@ -468,29 +512,31 @@
     fields, levels, arows, ncols = atmos.shape
     nk = n * ROWS8
     cells = (slots, CELLS)
+    packed = (slots // 2, 2 * CELLS)
     vmem = pltpu.VMEM
     hbm = pl.BlockSpec(memory_space=pl.ANY)
     local = pl.BlockSpec(memory_space=pltpu.VMEM)
-    kron = jnp.asarray(spread_weights())
+    spread, sides = jnp.asarray(spread_weights()), jnp.asarray(side_weights())
     return pl.pallas_call(
         functools.partial(kernel, n),
         out_shape=(
             jax.ShapeDtypeStruct(level_set.shape, F32),
             jax.ShapeDtypeStruct(atmos.shape, F32),
         ),
-        in_specs=[local, local, pl.BlockSpec(memory_space=pltpu.SMEM), hbm, hbm, hbm, hbm],
+        in_specs=[local, local, pl.BlockSpec(memory_space=pltpu.SMEM), hbm, hbm, hbm, hbm, hbm],
         out_specs=(hbm, hbm),
         scratch_shapes=[
-            vmem((LANES, CELLS), BF16),
+            vmem(spread.shape, BF16),
+            vmem(sides.shape, BF16),
             vmem(atmos.shape, F32),
             vmem(atmos.shape, F32),
-            vmem((2,) + cells, F32),
+            vmem(cells, F32),
+            vmem(packed, F32),
+            vmem(packed, F32),
             vmem(cells, jnp.int32),
-            vmem(cells, F32),
-            vmem(cells, F32),
-            vmem(cells, F32),
-            vmem(cells, F32),
-            vmem(cells, F32),
+        ]
+        + [vmem(packed, F32)] * 6
+        + [
             vmem((2, arows + 8, ncols), F32),
             vmem((LANES, arows // CPT * ncols), F32),
             vmem((nk, ncols), BF16),
@@ -501,7 +547,7 @@
         ]
         + [vmem((nk, LANES), F32)] * 6
         + [
-            pltpu.SemaphoreType.DMA((4,)),
+            pltpu.SemaphoreType.DMA((5,)),
             pltpu.SemaphoreType.DMA((2,)),
             pltpu.SemaphoreType.DMA((2, 2)),
             pltpu.SemaphoreType.DMA((2, 2)),
@@ -509,13 +555,14 @@
             pltpu.SemaphoreType.DMA((3,)),
         ],
         compiler_params=pltpu.CompilerParams(
-            collective_id=0, has_side_effects=True, vmem_limit_bytes=48 * 1024 * 1024
+            collective_id=0, has_side_effects=True, vmem_limit_bytes=62 * 1024 * 1024
         ),
     )(
         band_home.reshape(1, slots),
         band_tile.reshape(1, slots),
         fuel_table,
-        kron,
+        spread,
+        sides,
         atmos,
         level_set,
         fuel,

time: 37.1 us -> 27.5 us (0.74)
  Pallas kernels: 29.6 us -> 24 us
  local copies, waits for them, and re-layouts: 6.51 us -> 2.67 us
    pallas_call x1, Pallas kernels: 29.6 us -> 24 us  [shards(): pl.pallas_call(functools.partial(kernel, n), out_shape=(jax.ShapeDtypeStr...]
    unnamed x16 -> x4, local copies, waits for them, and re-layouts: 6.51 us -> 2.67 us
where the time goes in v1:
time: 27.5 us; the launch traced here: 27.4 us
  Pallas kernels  24 us (87%)
  local copies, waits for them, and re-layouts  2.67 us (10%)
  between operations  0.65 us (2%)
    pallas_call x1, Pallas kernels, shards(): pl.pallas_call(functools.partial(kernel, n), out_shape=(jax.ShapeDtypeStr...  24 us
    unnamed x4, local copies, waits for them, and re-layouts  2.67 us

profile of v1, /device:TPU:0, one launch (start us, length us, event | category | flops | bytes accessed | tf_op | source)
XLA Modules:
  0.0 27.4 jit_solution(2940564073923975494)
XLA Ops:
  0.6 24.0 %shard_map.95 = (f32[32,4096]{1,0:T(8,128)}, f32[3,4,8,1024]{3,2,1,0:T(8,128)}) custom-call(s32[1,32]{1,0:T(1,128)} %bitcast.2, s32[1,32]{1,0:T(1,128)} %bitcast.3, f32[3,13]{1,0:T(4,128)} %table_ref.1, bf16[256,768]{1,0:T(8,128)(2,1)} %constant.4.clone.spread_hbm, bf16[256,256]{1,0:T(8,128)(2,1)} %constant.5.clone.sides_hbm, f32[3,4,8,1024]{3,2,1,0:T(8,128)} %atmos_hbm.1, ...), custom_call_target="tpu_custom_call" | custom-call | tf_op jit(solution)/shard_map/pallas_call | solution.py:520
  24.7 0.0 copy-start
  24.7 1.9 %copy.12 = f32[32,4096]{1,0:T(8,128)} copy(f32[32,4096]{1,0:T(8,128)} %get-tuple-element.4) | data formatting | bytes 1048576
  26.6 0.0 copy-done
  26.6 0.7 %copy.13 = f32[3,4,8,1024]{3,2,1,0:T(8,128)} copy(f32[3,4,8,1024]{3,2,1,0:T(8,128)S(1)} %copy-done) | data formatting | bytes 786432
Async XLA Ops:
  24.7 1.9 %copy-start = (f32[3,4,8,1024]{3,2,1,0:T(8,128)S(1)}, f32[3,4,8,1024]{3,2,1,0:T(8,128)}, u32[]{:S(2)}) copy-start(f32[3,4,8,1024]{3,2,1,0:T(8,128)} %get-tuple-element.5) | copy-start | bytes 1179652
